TPU v7x, 32 devices: a whole 2x2x4 slice. The times are simulated.
32 devices in a mesh: dp: 4 (over y, x), rad: 4 (over z), azi: 2 (over core).
Axes of the slice: x: 2, y: 2, z: 4, core: 2. Of those that a mesh axis runs over, the one named last changes fastest.
Arguments:
- inputs: bfloat16 [4, 96, 16, 16, 256], P('dp', None, 'rad', 'azi'), may hold values from -6 to 6
- weight: bfloat16 [96, 2592], P('dp'), may hold values from -0.125 to 0.125
- bias: bfloat16 [96], P('dp'), may hold values from -3 to 3
- cotangent: bfloat16 [4, 96, 16, 16, 256], P('dp', None, 'rad', 'azi'), may hold values from -6 to 6
Outputs:
- output: bfloat16 [4, 96, 16, 16, 256], P('dp', None, 'rad', 'azi')
- input_grad: bfloat16 [4, 96, 16, 16, 256], P('dp', None, 'rad', 'azi')
- weight_grad: float32 [96, 2592], P('dp')
- bias_grad: float32 [96], P('dp')
All inputs are finite; a program needn't handle non-finite values.
Results may differ from a plain program's by a relative error of at most 0.015.
Values may be sent and summed in bfloat16 or wider, within the bound.
A program may use at most 128 MiB of HBM per device.

v0:
```python
import functools

import jax
import jax.numpy as jnp
from jax import lax
from jax.experimental import pallas as pl
from jax.experimental.pallas import tpu as pltpu
from jax.sharding import PartitionSpec as P

inverse_scale = 1.0 / 1024.0
VMEM_LIMIT = 60 * 1024 * 1024
LANES = 128
MESH = pl.DeviceIdType.MESH
F32, BF16 = jnp.float32, jnp.bfloat16


def shift(value, step, axis):
    extent = value.shape[axis]
    place = lax.broadcasted_iota(jnp.int32, value.shape, axis)
    edge = 0 if step == 1 else extent - 1
    return jnp.where(place == edge, 0.0, pltpu.roll(value, step % extent, axis))


def columns(cells, r, a):
    return jnp.concatenate([cells[r + i, a + j] for i in range(3) for j in range(3)], axis=0)


def convolve(weight, cells, r, a):
    stacked = jnp.dot(weight, columns(cells, r, a), preferred_element_type=F32)
    rows = stacked.shape[0] // 3
    return (
        stacked[rows:2 * rows]
        + shift(stacked[:rows], 1, 1)
        + shift(stacked[2 * rows:], -1, 1)
    )


class Halo:
    def __init__(self, cells, send, recv):
        self.cells, self.send, self.recv = cells, send, recv
        self.radial, self.azimuth = cells.shape[0] - 2, cells.shape[1] - 2
        self.rad, self.rads = lax.axis_index("rad"), lax.axis_size("rad")
        azi, azis = lax.axis_index("azi"), lax.axis_size("azi")
        self.next, self.prev = lax.rem(azi + 1, azis), lax.rem(azi + azis - 1, azis)

    def copy(self, slot, source, target, where):
        return pltpu.make_async_remote_copy(
            src_ref=source, dst_ref=target, send_sem=self.send.at[slot],
            recv_sem=self.recv.at[slot], device_id=where, device_id_type=MESH,
        )

    def azi_copies(self, first, rows):
        cells, last = self.cells, self.azimuth
        return [
            self.copy(first, cells.at[rows, last], cells.at[rows, 0], {"azi": self.next}),
            self.copy(first + 1, cells.at[rows, 1], cells.at[rows, last + 1], {"azi": self.prev}),
        ]

    def main(self):
        return self.azi_copies(0, pl.ds(1, self.radial))

    def up(self):
        span = pl.ds(1, self.azimuth)
        return self.copy(2, self.cells.at[self.radial, span], self.cells.at[0, span], {"rad": self.rad + 1})

    def down(self):
        span = pl.ds(1, self.azimuth)
        return self.copy(
            3, self.cells.at[1, span], self.cells.at[self.radial + 1, span], {"rad": self.rad - 1}
        )

    def start(self):
        @pl.when(self.rad < self.rads - 1)
        def _():
            self.up().start()

        @pl.when(self.rad > 0)
        def _():
            self.down().start()

        for copy in self.main():
            copy.start()

    def wait_main(self):
        for copy in self.main():
            copy.wait()

    def finish_rim(self):
        @pl.when(self.rad > 0)
        def _():
            self.up().wait_recv()
            for copy in self.azi_copies(4, 0):
                copy.start()

        @pl.when(self.rad < self.rads - 1)
        def _():
            self.down().wait_recv()
            for copy in self.azi_copies(6, self.radial + 1):
                copy.start()

        @pl.when(self.rad == 0)
        def _():
            self.cells[0] = jnp.zeros(self.cells.shape[1:], BF16)

        @pl.when(self.rad == self.rads - 1)
        def _():
            self.cells[self.radial + 1] = jnp.zeros(self.cells.shape[1:], BF16)

        @pl.when(self.rad > 0)
        def _():
            self.down().wait_send()
            for copy in self.azi_copies(4, 0):
                copy.wait()

        @pl.when(self.rad < self.rads - 1)
        def _():
            self.up().wait_send()
            for copy in self.azi_copies(6, self.radial + 1):
                copy.wait()


def kernel(
    field, weight, bias, cotangent,
    output, input_grad, weight_grad, bias_grad,
    cells, dcells, turned, result, dturned, total, bias_total,
    mine, slots, fwd_weight, back_weight, bias_column, part_out, part_in, piece_out, piece_in, final,
    halo_send, halo_recv, dhalo_send, dhalo_recv, w_send, w_recv, p_send, p_recv, q_send, q_recv, f_send, f_recv,
):
    channels, radial, azimuth, axial = field.shape
    dp, dps = lax.axis_index("dp"), lax.axis_size("dp")
    rad, azi, azis = lax.axis_index("rad"), lax.axis_index("azi"), lax.axis_size("azi")
    peers = lax.axis_size("rad") * azis
    me = rad * azis + azi
    rows, depth = weight.shape
    outs = rows * dps
    block = depth // 27
    width = final.shape[2]
    span = (mine.shape[1] - LANES) // 3

    def group(k):
        return lax.rem(dp + k, dps)

    def peer(k):
        other = lax.rem(me + k, peers)
        return {"rad": other // azis, "azi": lax.rem(other, azis)}

    barrier = pltpu.get_barrier_semaphore()

    @pl.loop(1, dps)
    def _(k):
        pl.semaphore_signal(barrier, inc=1, device_id={"dp": group(k)}, device_id_type=MESH)

    @pl.loop(1, peers)
    def _(k):
        pl.semaphore_signal(barrier, inc=1, device_id=peer(k), device_id_type=MESH)

    own = weight[...].astype(F32)
    pad = jnp.zeros((rows, span - 9 * block), F32)
    for k in range(3):
        parts = [own[:, t * block:(t + 1) * block] for t in range(k, 27, 3)]
        mine[:, LANES + k * span:LANES + (k + 1) * span] = jnp.concatenate(parts + [pad], axis=1).astype(BF16)
    row = lax.broadcasted_iota(jnp.int32, (rows, rows), 0)
    col = lax.broadcasted_iota(jnp.int32, (rows, rows), 1)
    column = jnp.sum(jnp.where(row == col, bias[...].astype(F32), 0.0), axis=1, keepdims=True)
    mine[:, :LANES] = jnp.broadcast_to(column, (rows, LANES)).astype(BF16)

    @pl.loop(0, radial)
    def _(r):
        cells[r + 1, pl.ds(1, azimuth)] = jnp.swapaxes(field[:, r], 0, 1)

    pl.semaphore_wait(barrier, dps + peers - 2)

    def w_copy(k):
        return pltpu.make_async_remote_copy(
            src_ref=mine, dst_ref=slots.at[dp], send_sem=w_send.at[k], recv_sem=w_recv.at[k],
            device_id={"dp": group(k)}, device_id_type=MESH,
        )

    halo = Halo(cells, halo_send, halo_recv)

    @pl.loop(1, dps)
    def _(k):
        w_copy(k).start()

    halo.start()
    slots[dp] = mine[...]
    total[...] = jnp.zeros_like(total)
    bias_total[...] = jnp.zeros_like(bias_total)
    halo.wait_main()

    @pl.loop(1, dps)
    def _(k):
        w_copy(k).wait()

    gathered = jnp.concatenate([slots[g].astype(F32) for g in range(dps)], axis=0)
    bias_column[...] = gathered[:, :LANES]
    for k in range(3):
        start = LANES + k * span
        part = gathered[:, start:start + 9 * block]
        fwd_weight[k * outs:(k + 1) * outs] = part.astype(BF16)
        flipped = [part[:, t * block:(t + 1) * block] for t in reversed(range(9))]
        back_weight[(2 - k) * channels:(3 - k) * channels] = (
            jnp.concatenate(flipped, axis=0).T.astype(BF16)
        )

    @pl.loop(0, radial)
    def _(n):
        r = lax.rem(n + 1, radial)

        @pl.when(n == radial - 2)
        def _():
            halo.finish_rim()

        turned[...] = jnp.swapaxes(cotangent[:, r], 0, 1)

        @pl.loop(0, azimuth // 2)
        def _(pair):
            for p in range(2):
                a = 2 * pair + p
                preact = convolve(fwd_weight[...], cells, r, a) + bias_column[:, :1]
                gate = 0.5 * jnp.tanh(0.5 * preact) + 0.5
                result[a] = (preact * gate).astype(BF16)
                d = turned[a].astype(F32) * gate * (1.0 + preact * (1.0 - gate))
                d16 = d.astype(BF16)
                d = d16.astype(F32)
                dcells[r + 1, a + 1] = d16
                bias_total[...] += d
                flat = jnp.concatenate([d, jnp.zeros((LANES - outs, axial), F32)], axis=0).T
                dturned[a, pl.ds(pl.multiple_of(r * axial, axial), axial)] = jnp.concatenate(
                    [shift(flat, -1, 0), flat, shift(flat, 1, 0)], axis=1
                ).astype(BF16)

        output[:, r] = jnp.swapaxes(result[...], 0, 1)

    dhalo = Halo(dcells, dhalo_send, dhalo_recv)
    dhalo.start()

    @pl.loop(0, azimuth)
    def _(a):
        right = dturned[a]
        for i in range(3):
            left = jnp.concatenate(
                [jnp.concatenate([cells[r + i, a + j] for j in range(3)], axis=0) for r in range(radial)],
                axis=1,
            )
            total[i] += jnp.dot(left, right, preferred_element_type=F32)

    dhalo.wait_main()
    dhalo.finish_rim()

    taps = [
        total[i, j * channels:(j + 1) * channels, k * LANES:(k + 1) * LANES]
        for i in range(3) for j in range(3) for k in range(3)
    ]
    grads = jnp.concatenate(taps, axis=0).T[:outs] * inverse_scale
    bias_sum = jnp.sum(bias_total[...], axis=1, keepdims=True) * inverse_scale
    fill = -(-depth // LANES) * LANES
    spare = peers * width - fill - LANES
    grads = jnp.concatenate(
        [grads, jnp.zeros((outs, fill - depth), F32), jnp.broadcast_to(bias_sum, (outs, LANES))]
        + ([jnp.zeros((outs, spare), F32)] if spare else []),
        axis=1,
    )
    for g in range(dps):
        for p in range(peers):
            part_out[g, p] = grads[g * rows:(g + 1) * rows, p * width:(p + 1) * width].astype(BF16)

    def p_copy(k):
        return pltpu.make_async_remote_copy(
            src_ref=part_out.at[group(k)], dst_ref=part_in.at[k], send_sem=p_send.at[k],
            recv_sem=p_recv.at[k], device_id={"dp": group(k)}, device_id_type=MESH,
        )

    def q_copy(k):
        return pltpu.make_async_remote_copy(
            src_ref=piece_out.at[lax.rem(me + k, peers)], dst_ref=piece_in.at[k], send_sem=q_send.at[k],
            recv_sem=q_recv.at[k], device_id=peer(k), device_id_type=MESH,
        )

    def f_copy(k):
        return pltpu.make_async_remote_copy(
            src_ref=final.at[me], dst_ref=final.at[me], send_sem=f_send.at[k],
            recv_sem=f_recv.at[k], device_id=peer(k), device_id_type=MESH,
        )

    @pl.loop(1, dps)
    def _(k):
        p_copy(k).start()

    @pl.loop(0, radial)
    def _(r):
        @pl.when(r == 1)
        def _():
            @pl.loop(1, dps)
            def _(k):
                p_copy(k).wait()

            @pl.loop(0, peers)
            def _(p):
                term = part_out[dp, p].astype(F32)
                for k in range(1, dps):
                    term = term + part_in[k, p].astype(F32)
                piece_out[p] = term.astype(BF16)

            @pl.loop(1, peers)
            def _(k):
                q_copy(k).start()

        @pl.when(r == radial - 1)
        def _():
            @pl.loop(1, peers)
            def _(k):
                q_copy(k).wait()

            term = piece_out[me].astype(F32)
            for k in range(1, peers):
                term = term + piece_in[k].astype(F32)
            final[me] = term.astype(BF16)

            @pl.loop(1, peers)
            def _(k):
                f_copy(k).start()

        @pl.loop(0, azimuth // 2)
        def _(pair):
            for p in range(2):
                a = 2 * pair + p
                result[a] = convolve(back_weight[...], dcells, r, a).astype(BF16)

        input_grad[:, r] = jnp.swapaxes(result[...], 0, 1)

    @pl.loop(1, peers)
    def _(k):
        f_copy(k).wait()

    for p in range(peers):
        stop = min(depth, (p + 1) * width)
        if stop > p * width:
            weight_grad[:, p * width:stop] = final[p].astype(F32)[:, :stop - p * width]
        if p * width <= fill < (p + 1) * width:
            column = final[p, :, fill - p * width:fill - p * width + LANES].astype(F32)[:, :1]
            bias_grad[...] = jnp.sum(jnp.where(row == col, column, 0.0), axis=0, keepdims=True)


def on_device(inputs, weight, bias, cotangent):
    _, channels, radial, azimuth, axial = inputs.shape
    rows, depth = weight.shape
    dps, peers = lax.axis_size("dp"), lax.axis_size("rad") * lax.axis_size("azi")
    outs = rows * dps
    tiles = -(-depth // LANES) + 1
    width = -(-tiles // peers) * LANES
    span = -(-depth // 3 // LANES) * LANES
    vmem = pl.BlockSpec(memory_space=pltpu.VMEM)
    shape = jax.ShapeDtypeStruct
    dma = pltpu.SemaphoreType.DMA
    output, input_grad, weight_grad, bias_grad = pl.pallas_call(
        kernel,
        out_shape=(
            shape((outs, radial, azimuth, axial), BF16),
            shape((channels, radial, azimuth, axial), BF16),
            shape((rows, depth), F32),
            shape((1, rows), F32),
        ),
        in_specs=[vmem] * 4,
        out_specs=(vmem,) * 4,
        scratch_shapes=[
            pltpu.VMEM((radial + 2, azimuth + 2, channels, axial), BF16),
            pltpu.VMEM((radial + 2, azimuth + 2, outs, axial), BF16),
            pltpu.VMEM((azimuth, outs, axial), BF16),
            pltpu.VMEM((azimuth, outs, axial), BF16),
            pltpu.VMEM((azimuth, radial * axial, 3 * LANES), BF16),
            pltpu.VMEM((3, 3 * channels, 3 * LANES), F32),
            pltpu.VMEM((outs, axial), F32),
            pltpu.VMEM((rows, LANES + 3 * span), BF16),
            pltpu.VMEM((dps, rows, LANES + 3 * span), BF16),
            pltpu.VMEM((3 * outs, 9 * channels), BF16),
            pltpu.VMEM((3 * channels, 9 * outs), BF16),
            pltpu.VMEM((outs, LANES), F32),
            pltpu.VMEM((dps, peers, rows, width), BF16),
            pltpu.VMEM((dps, peers, rows, width), BF16),
            pltpu.VMEM((peers, rows, width), BF16),
            pltpu.VMEM((peers, rows, width), BF16),
            pltpu.VMEM((peers, rows, width), BF16),
            dma((8,)), dma((8,)), dma((8,)), dma((8,)),
            dma((dps,)), dma((dps,)), dma((dps,)), dma((dps,)),
            dma((peers,)), dma((peers,)), dma((peers,)), dma((peers,)),
        ],
        compiler_params=pltpu.CompilerParams(
            vmem_limit_bytes=VMEM_LIMIT, collective_id=0, has_side_effects=True
        ),
    )(inputs[0], weight, bias[None], cotangent[0])
    return output[None], input_grad[None], weight_grad, bias_grad[0]


def solution(mesh):
    field_spec = P("dp", None, "rad", "azi", None)
    return jax.shard_map(
        on_device,
        mesh=mesh,
        in_specs=(field_spec, P("dp", None), P("dp"), field_spec),
        out_specs=(field_spec, field_spec, P("dp", None), P("dp")),
        check_vma=False,
    )
```

profile of v0, /device:TPU:0, one launch (start us, length us, event | category | flops | bytes accessed | tf_op | source)
XLA Modules:
  0.0 69.8 jit_solution(4405391464710941039)
XLA Ops:
  0.6 64.0 %shard_map.75 = (bf16[96,4,8,256]{3,2,1,0:T(8,128)(2,1)}, bf16[96,4,8,256]{3,2,1,0:T(8,128)(2,1)}, f32[24,2592]{1,0:T(8,128)}, f32[1,24]{1,0:T(1,128)}) custom-call(bf16[96,4,8,256]{3,2,1,0:T(8,128)(2,1)} %bitcast.6, bf16[24,2592]{1,0:T(8,128)(2,1)} %weight.1, bf16[1,24]{1,0:T(2,128)(2,1)} %bitcast.10, bf16[96,4,8,256]{3,2,1,0:T(8,128)(2,1)} %bitcast.7), custom_call_target="tpu_custom_call" | custom-call | tf_op jit(solution)/shard_map/pallas_call | solution.py:356
  64.6 0.0 copy-start
  64.6 2.8 %copy.12 = bf16[1,96,4,8,256]{4,3,2,1,0:T(8,128)(2,1)} copy(bf16[1,96,4,8,256]{4,3,2,1,0:T(8,128)(2,1)} %bitcast.9) | data formatting | bytes 3145728
  67.4 0.0 copy-done
  67.4 0.0 copy-start.1
  67.4 0.0 copy-start.2
  67.4 1.1 %copy.13 = bf16[1,96,4,8,256]{4,3,2,1,0:T(8,128)(2,1)} copy(bf16[1,96,4,8,256]{4,3,2,1,0:T(8,128)(2,1)S(1)} %bitcast.8) | data formatting | bytes 3145728
  68.6 0.1 copy-done.1
  68.6 0.7 copy.14
  69.3 0.0 copy-done.2
  69.3 0.5 copy.15
Async XLA Ops:
  64.6 2.8 %copy-start = (bf16[96,4,8,256]{3,2,1,0:T(8,128)(2,1)S(1)}, bf16[96,4,8,256]{3,2,1,0:T(8,128)(2,1)}, u32[]{:S(2)}) copy-start(bf16[96,4,8,256]{3,2,1,0:T(8,128)(2,1)} %get-tuple-element.9) | copy-start | bytes 4718596
  67.4 1.2 %copy-start.1 = (f32[24,2592]{1,0:T(8,128)S(1)}, f32[24,2592]{1,0:T(8,128)}, u32[]{:S(2)}) copy-start(f32[24,2592]{1,0:T(8,128)} %get-tuple-element.18) | copy-start | bytes 746500
  67.4 1.9 %copy-start.2 = (f32[1,24]{1,0:T(1,128)S(1)}, f32[1,24]{1,0:T(1,128)}, u32[]{:S(2)}) copy-start(f32[1,24]{1,0:T(1,128)} %get-tuple-element.11) | copy-start | bytes 292
where the time goes:
time: 70 us; the launch traced here: 69.8 us
  Pallas kernels  64 us (91%)
  local copies, waits for them, and re-layouts  5.21 us (7%)
    pallas_call x1, Pallas kernels, on_device(): pl.pallas_call(kernel, out_shape=(shape((outs, radial, azimuth, axial), B...  64 us
    unnamed x10, local copies, waits for them, and re-layouts  5.21 us

commit v1 on v0

--- a/solution.py
+++ b/solution.py
@@ -122,9 +122,10 @@
 def kernel(
     field, weight, bias, cotangent,
     output, input_grad, weight_grad, bias_grad,
-    cells, dcells, turned, result, dturned, total, bias_total,
+    cells, dcells, given, turned, result, back_result, dturned, total, bias_total,
     mine, slots, fwd_weight, back_weight, bias_column, part_out, part_in, piece_out, piece_in, final,
     halo_send, halo_recv, dhalo_send, dhalo_recv, w_send, w_recv, p_send, p_recv, q_send, q_recv, f_send, f_recv,
+    in_sem, out_sem, back_sem,
 ):
     channels, radial, azimuth, axial = field.shape
     dp, dps = lax.axis_index("dp"), lax.axis_size("dp")
@@ -144,7 +145,16 @@
         other = lax.rem(me + k, peers)
         return {"rad": other // azis, "azi": lax.rem(other, azis)}
 
+    def out_copy(r):
+        return pltpu.make_async_copy(result.at[r], output.at[r], out_sem.at[r])
+
+    def back_copy(r):
+        return pltpu.make_async_copy(back_result.at[r], input_grad.at[r], back_sem.at[r])
+
     barrier = pltpu.get_barrier_semaphore()
+
+    given_copy = pltpu.make_async_copy(cotangent, given, in_sem)
+    given_copy.start()
 
     @pl.loop(1, dps)
     def _(k):
@@ -186,6 +196,12 @@
     slots[dp] = mine[...]
     total[...] = jnp.zeros_like(total)
     bias_total[...] = jnp.zeros_like(bias_total)
+    given_copy.wait()
+
+    @pl.loop(0, radial)
+    def _(r):
+        turned[r] = jnp.swapaxes(given[:, r], 0, 1)
+
     halo.wait_main()
 
     @pl.loop(1, dps)
@@ -211,16 +227,14 @@
         def _():
             halo.finish_rim()
 
-        turned[...] = jnp.swapaxes(cotangent[:, r], 0, 1)
-
         @pl.loop(0, azimuth // 2)
         def _(pair):
             for p in range(2):
                 a = 2 * pair + p
                 preact = convolve(fwd_weight[...], cells, r, a) + bias_column[:, :1]
                 gate = 0.5 * jnp.tanh(0.5 * preact) + 0.5
-                result[a] = (preact * gate).astype(BF16)
-                d = turned[a].astype(F32) * gate * (1.0 + preact * (1.0 - gate))
+                result[r, a] = (preact * gate).astype(BF16)
+                d = turned[r, a].astype(F32) * gate * (1.0 + preact * (1.0 - gate))
                 d16 = d.astype(BF16)
                 d = d16.astype(F32)
                 dcells[r + 1, a + 1] = d16
@@ -230,7 +244,7 @@
                     [shift(flat, -1, 0), flat, shift(flat, 1, 0)], axis=1
                 ).astype(BF16)
 
-        output[:, r] = jnp.swapaxes(result[...], 0, 1)
+        out_copy(r).start()
 
     dhalo = Halo(dcells, dhalo_send, dhalo_recv)
     dhalo.start()
@@ -244,9 +258,6 @@
                 axis=1,
             )
             total[i] += jnp.dot(left, right, preferred_element_type=F32)
-
-    dhalo.wait_main()
-    dhalo.finish_rim()
 
     taps = [
         total[i, j * channels:(j + 1) * channels, k * LANES:(k + 1) * LANES]
@@ -287,9 +298,20 @@
     def _(k):
         p_copy(k).start()
 
-    @pl.loop(0, radial)
-    def _(r):
-        @pl.when(r == 1)
+    dhalo.wait_main()
+    pairs = azimuth // 2
+    steps = radial * pairs
+
+    @pl.loop(0, steps)
+    def _(step):
+        r = lax.rem(step // pairs + 1, radial)
+        pair = lax.rem(step, pairs)
+
+        @pl.when(step == (radial - 2) * pairs)
+        def _():
+            dhalo.finish_rim()
+
+        @pl.when(step == steps // 2)
         def _():
             @pl.loop(1, dps)
             def _(k):
@@ -306,7 +328,7 @@
             def _(k):
                 q_copy(k).start()
 
-        @pl.when(r == radial - 1)
+        @pl.when(step == 3 * steps // 4)
         def _():
             @pl.loop(1, peers)
             def _(k):
@@ -321,13 +343,13 @@
             def _(k):
                 f_copy(k).start()
 
-        @pl.loop(0, azimuth // 2)
-        def _(pair):
-            for p in range(2):
-                a = 2 * pair + p
-                result[a] = convolve(back_weight[...], dcells, r, a).astype(BF16)
-
-        input_grad[:, r] = jnp.swapaxes(result[...], 0, 1)
+        for p in range(2):
+            a = 2 * pair + p
+            back_result[r, a] = convolve(back_weight[...], dcells, r, a).astype(BF16)
+
+        @pl.when(pair == pairs - 1)
+        def _():
+            back_copy(r).start()
 
     @pl.loop(1, peers)
     def _(k):
@@ -340,6 +362,11 @@
         if p * width <= fill < (p + 1) * width:
             column = final[p, :, fill - p * width:fill - p * width + LANES].astype(F32)[:, :1]
             bias_grad[...] = jnp.sum(jnp.where(row == col, column, 0.0), axis=0, keepdims=True)
+
+    @pl.loop(0, radial)
+    def _(r):
+        out_copy(r).wait()
+        back_copy(r).wait()
 
 
 def on_device(inputs, weight, bias, cotangent):
@@ -351,23 +378,26 @@
     width = -(-tiles // peers) * LANES
     span = -(-depth // 3 // LANES) * LANES
     vmem = pl.BlockSpec(memory_space=pltpu.VMEM)
+    anywhere = pl.BlockSpec(memory_space=pl.ANY)
     shape = jax.ShapeDtypeStruct
     dma = pltpu.SemaphoreType.DMA
     output, input_grad, weight_grad, bias_grad = pl.pallas_call(
         kernel,
         out_shape=(
-            shape((outs, radial, azimuth, axial), BF16),
-            shape((channels, radial, azimuth, axial), BF16),
+            shape((radial, azimuth, outs, axial), BF16),
+            shape((radial, azimuth, channels, axial), BF16),
             shape((rows, depth), F32),
             shape((1, rows), F32),
         ),
-        in_specs=[vmem] * 4,
-        out_specs=(vmem,) * 4,
+        in_specs=[vmem] * 3 + [anywhere],
+        out_specs=(anywhere, anywhere, vmem, vmem),
         scratch_shapes=[
             pltpu.VMEM((radial + 2, azimuth + 2, channels, axial), BF16),
             pltpu.VMEM((radial + 2, azimuth + 2, outs, axial), BF16),
-            pltpu.VMEM((azimuth, outs, axial), BF16),
-            pltpu.VMEM((azimuth, outs, axial), BF16),
+            pltpu.VMEM((outs, radial, azimuth, axial), BF16),
+            pltpu.VMEM((radial, azimuth, outs, axial), BF16),
+            pltpu.VMEM((radial, azimuth, outs, axial), BF16),
+            pltpu.VMEM((radial, azimuth, channels, axial), BF16),
             pltpu.VMEM((azimuth, radial * axial, 3 * LANES), BF16),
             pltpu.VMEM((3, 3 * channels, 3 * LANES), F32),
             pltpu.VMEM((outs, axial), F32),
@@ -384,12 +414,15 @@
             dma((8,)), dma((8,)), dma((8,)), dma((8,)),
             dma((dps,)), dma((dps,)), dma((dps,)), dma((dps,)),
             dma((peers,)), dma((peers,)), dma((peers,)), dma((peers,)),
+            dma, dma((radial,)), dma((radial,)),
         ],
         compiler_params=pltpu.CompilerParams(
             vmem_limit_bytes=VMEM_LIMIT, collective_id=0, has_side_effects=True
         ),
     )(inputs[0], weight, bias[None], cotangent[0])
-    return output[None], input_grad[None], weight_grad, bias_grad[0]
+    output = output.transpose(2, 0, 1, 3)[None]
+    input_grad = input_grad.transpose(2, 0, 1, 3)[None]
+    return output, input_grad, weight_grad, bias_grad[0]
 
 
 def solution(mesh):

time: 70 us -> 66.1 us (0.944)
  Pallas kernels: 64 us -> 58.5 us
  local copies, waits for them, and re-layouts: 5.21 us -> 6.8 us
    pallas_call x1, Pallas kernels: 64 us -> 58.5 us  [on_device(): pl.pallas_call(kernel, out_shape=(shape((radial, azimuth, outs, axial), B...]
    unnamed x10, local copies, waits for them, and re-layouts: 5.21 us -> 6.8 us
where the time goes in v1:
time: 66.1 us; the launch traced here: 66 us
  Pallas kernels  58.5 us (89%)
  local copies, waits for them, and re-layouts  6.8 us (10%)
    pallas_call x1, Pallas kernels, on_device(): pl.pallas_call(kernel, out_shape=(shape((radial, azimuth, outs, axial), B...  58.5 us
    unnamed x10, local copies, waits for them, and re-layouts  6.8 us

profile of v1, /device:TPU:0, one launch (start us, length us, event | category | flops | bytes accessed | tf_op | source)
XLA Modules:
  0.0 66.0 jit_solution(6750587587695043537)
XLA Ops:
  0.6 58.5 %shard_map.75 = (bf16[4,8,96,256]{3,2,1,0:T(8,128)(2,1)}, bf16[4,8,96,256]{3,2,1,0:T(8,128)(2,1)}, f32[24,2592]{1,0:T(8,128)}, f32[1,24]{1,0:T(1,128)}) custom-call(bf16[96,4,8,256]{3,2,1,0:T(8,128)(2,1)} %bitcast.10, bf16[24,2592]{1,0:T(8,128)(2,1)} %weight.1, bf16[1,24]{1,0:T(2,128)(2,1)} %bitcast.14, bf16[96,4,8,256]{3,2,1,0:T(8,128)(2,1)} %bitcast.11), custom_call_target="tpu_custom_call" | custom-call | tf_op jit(solution)/shard_map/pallas_call | solution.py:384
  59.2 0.0 copy-start
  59.2 3.5 %copy.8 = bf16[1,96,4,8,256]{4,3,2,1,0:T(8,128)(2,1)} copy(bf16[1,96,4,8,256]{4,1,3,2,0:T(8,128)(2,1)} %bitcast.13) | data formatting | bytes 3145728
  62.7 0.0 copy-done
  62.7 0.0 copy-start.1
  62.7 0.0 copy-start.2
  62.7 2.0 %copy.9 = bf16[1,96,4,8,256]{4,3,2,1,0:T(8,128)(2,1)} copy(bf16[1,96,4,8,256]{4,1,3,2,0:T(8,128)(2,1)S(1)} %bitcast.12) | data formatting | bytes 3145728
  64.8 0.0 copy-done.1
  64.8 0.7 %copy.12 = f32[24,2592]{1,0:T(8,128)} copy(f32[24,2592]{1,0:T(8,128)S(1)} %copy-done.1) | data formatting | bytes 497664
  65.5 0.0 copy-done.2
  65.5 0.5 copy.13
Async XLA Ops:
  59.2 3.6 %copy-start = (bf16[4,8,96,256]{3,2,1,0:T(8,128)(2,1)S(1)}, bf16[4,8,96,256]{3,2,1,0:T(8,128)(2,1)}, u32[]{:S(2)}) copy-start(bf16[4,8,96,256]{3,2,1,0:T(8,128)(2,1)} %get-tuple-element.9) | copy-start | bytes 4718596
  62.7 2.0 %copy-start.1 = (f32[24,2592]{1,0:T(8,128)S(1)}, f32[24,2592]{1,0:T(8,128)}, u32[]{:S(2)}) copy-start(f32[24,2592]{1,0:T(8,128)} %get-tuple-element.22) | copy-start | bytes 746500
  62.7 2.7 %copy-start.2 = (f32[1,24]{1,0:T(1,128)S(1)}, f32[1,24]{1,0:T(1,128)}, u32[]{:S(2)}) copy-start(f32[1,24]{1,0:T(1,128)} %get-tuple-element.11) | copy-start | bytes 292

commit v2 on v1

--- a/solution.py
+++ b/solution.py
@@ -69,7 +69,7 @@
             3, self.cells.at[1, span], self.cells.at[self.radial + 1, span], {"rad": self.rad - 1}
         )
 
-    def start(self):
+    def start_rad(self):
         @pl.when(self.rad < self.rads - 1)
         def _():
             self.up().start()
@@ -78,6 +78,7 @@
         def _():
             self.down().start()
 
+    def start_main(self):
         for copy in self.main():
             copy.start()
 
@@ -174,10 +175,11 @@
     column = jnp.sum(jnp.where(row == col, bias[...].astype(F32), 0.0), axis=1, keepdims=True)
     mine[:, :LANES] = jnp.broadcast_to(column, (rows, LANES)).astype(BF16)
 
-    @pl.loop(0, radial)
-    def _(r):
+    def turn_row(r):
         cells[r + 1, pl.ds(1, azimuth)] = jnp.swapaxes(field[:, r], 0, 1)
 
+    turn_row(0)
+    turn_row(radial - 1)
     pl.semaphore_wait(barrier, dps + peers - 2)
 
     def w_copy(k):
@@ -192,7 +194,13 @@
     def _(k):
         w_copy(k).start()
 
-    halo.start()
+    halo.start_rad()
+
+    @pl.loop(1, radial - 1)
+    def _(r):
+        turn_row(r)
+
+    halo.start_main()
     slots[dp] = mine[...]
     total[...] = jnp.zeros_like(total)
     bias_total[...] = jnp.zeros_like(bias_total)
@@ -247,40 +255,38 @@
         out_copy(r).start()
 
     dhalo = Halo(dcells, dhalo_send, dhalo_recv)
-    dhalo.start()
-
-    @pl.loop(0, azimuth)
-    def _(a):
-        right = dturned[a]
-        for i in range(3):
+    dhalo.start_rad()
+    dhalo.start_main()
+
+    def p_copy(i, k):
+        return pltpu.make_async_remote_copy(
+            src_ref=part_out.at[i, group(k)], dst_ref=part_in.at[i, k], send_sem=p_send.at[i, k],
+            recv_sem=p_recv.at[i, k], device_id={"dp": group(k)}, device_id_type=MESH,
+        )
+
+    third = 9 * block
+    bias_sum = jnp.sum(bias_total[...], axis=1, keepdims=True) * inverse_scale
+    for i in range(3):
+        @pl.loop(0, azimuth)
+        def _(a):
             left = jnp.concatenate(
                 [jnp.concatenate([cells[r + i, a + j] for j in range(3)], axis=0) for r in range(radial)],
                 axis=1,
             )
-            total[i] += jnp.dot(left, right, preferred_element_type=F32)
-
-    taps = [
-        total[i, j * channels:(j + 1) * channels, k * LANES:(k + 1) * LANES]
-        for i in range(3) for j in range(3) for k in range(3)
-    ]
-    grads = jnp.concatenate(taps, axis=0).T[:outs] * inverse_scale
-    bias_sum = jnp.sum(bias_total[...], axis=1, keepdims=True) * inverse_scale
-    fill = -(-depth // LANES) * LANES
-    spare = peers * width - fill - LANES
-    grads = jnp.concatenate(
-        [grads, jnp.zeros((outs, fill - depth), F32), jnp.broadcast_to(bias_sum, (outs, LANES))]
-        + ([jnp.zeros((outs, spare), F32)] if spare else []),
-        axis=1,
-    )
-    for g in range(dps):
-        for p in range(peers):
-            part_out[g, p] = grads[g * rows:(g + 1) * rows, p * width:(p + 1) * width].astype(BF16)
-
-    def p_copy(k):
-        return pltpu.make_async_remote_copy(
-            src_ref=part_out.at[group(k)], dst_ref=part_in.at[k], send_sem=p_send.at[k],
-            recv_sem=p_recv.at[k], device_id={"dp": group(k)}, device_id_type=MESH,
-        )
+            total[i] += jnp.dot(left, dturned[a], preferred_element_type=F32)
+
+        taps = [
+            total[i, j * channels:(j + 1) * channels, k * LANES:(k + 1) * LANES]
+            for j in range(3) for k in range(3)
+        ]
+        grads = jnp.concatenate(taps, axis=0).T[:outs] * inverse_scale
+        grads = jnp.concatenate([grads, jnp.broadcast_to(bias_sum, (outs, span - third))], axis=1)
+        for g in range(dps):
+            part_out[i, g] = grads[g * rows:(g + 1) * rows].astype(BF16)
+
+        @pl.loop(1, dps)
+        def _(k):
+            p_copy(i, k).start()
 
     def q_copy(k):
         return pltpu.make_async_remote_copy(
@@ -294,10 +300,6 @@
             recv_sem=f_recv.at[k], device_id=peer(k), device_id_type=MESH,
         )
 
-    @pl.loop(1, dps)
-    def _(k):
-        p_copy(k).start()
-
     dhalo.wait_main()
     pairs = azimuth // 2
     steps = radial * pairs
@@ -311,24 +313,30 @@
         def _():
             dhalo.finish_rim()
 
-        @pl.when(step == steps // 2)
-        def _():
-            @pl.loop(1, dps)
-            def _(k):
-                p_copy(k).wait()
-
-            @pl.loop(0, peers)
-            def _(p):
-                term = part_out[dp, p].astype(F32)
+        @pl.when(step == 3 * steps // 8)
+        def _():
+            terms = []
+            for i in range(3):
+                @pl.loop(1, dps)
+                def _(k):
+                    p_copy(i, k).wait()
+
+                term = part_out[i, dp].astype(F32)
                 for k in range(1, dps):
-                    term = term + part_in[k, p].astype(F32)
-                piece_out[p] = term.astype(BF16)
+                    term = term + part_in[i, k].astype(F32)
+                terms.append(term)
+            spare = peers * width - 3 * span
+            if spare:
+                terms.append(jnp.zeros((rows, spare), F32))
+            terms = jnp.concatenate(terms, axis=1).astype(BF16)
+            for p in range(peers):
+                piece_out[p] = terms[:, p * width:(p + 1) * width]
 
             @pl.loop(1, peers)
             def _(k):
                 q_copy(k).start()
 
-        @pl.when(step == 3 * steps // 4)
+        @pl.when(step == 11 * steps // 16)
         def _():
             @pl.loop(1, peers)
             def _(k):
@@ -355,13 +363,13 @@
     def _(k):
         f_copy(k).wait()
 
-    for p in range(peers):
-        stop = min(depth, (p + 1) * width)
-        if stop > p * width:
-            weight_grad[:, p * width:stop] = final[p].astype(F32)[:, :stop - p * width]
-        if p * width <= fill < (p + 1) * width:
-            column = final[p, :, fill - p * width:fill - p * width + LANES].astype(F32)[:, :1]
-            bias_grad[...] = jnp.sum(jnp.where(row == col, column, 0.0), axis=0, keepdims=True)
+    used = -(-3 * span // width)
+    whole = jnp.concatenate([final[p].astype(F32) for p in range(used)], axis=1)
+    weight_grad[...] = jnp.concatenate(
+        [whole[:, i * span:i * span + third] for i in range(3)], axis=1
+    )
+    column = whole[:, 2 * span + third:2 * span + third + 1]
+    bias_grad[...] = jnp.sum(jnp.where(row == col, column, 0.0), axis=0, keepdims=True)
 
     @pl.loop(0, radial)
     def _(r):
@@ -374,9 +382,8 @@
     rows, depth = weight.shape
     dps, peers = lax.axis_size("dp"), lax.axis_size("rad") * lax.axis_size("azi")
     outs = rows * dps
-    tiles = -(-depth // LANES) + 1
-    width = -(-tiles // peers) * LANES
-    span = -(-depth // 3 // LANES) * LANES
+    span = -(-(depth // 3 + 1) // LANES) * LANES
+    width = -(-3 * span // LANES // peers) * LANES
     vmem = pl.BlockSpec(memory_space=pltpu.VMEM)
     anywhere = pl.BlockSpec(memory_space=pl.ANY)
     shape = jax.ShapeDtypeStruct
@@ -406,13 +413,13 @@
             pltpu.VMEM((3 * outs, 9 * channels), BF16),
             pltpu.VMEM((3 * channels, 9 * outs), BF16),
             pltpu.VMEM((outs, LANES), F32),
-            pltpu.VMEM((dps, peers, rows, width), BF16),
-            pltpu.VMEM((dps, peers, rows, width), BF16),
+            pltpu.VMEM((3, dps, rows, span), BF16),
+            pltpu.VMEM((3, dps, rows, span), BF16),
             pltpu.VMEM((peers, rows, width), BF16),
             pltpu.VMEM((peers, rows, width), BF16),
             pltpu.VMEM((peers, rows, width), BF16),
             dma((8,)), dma((8,)), dma((8,)), dma((8,)),
-            dma((dps,)), dma((dps,)), dma((dps,)), dma((dps,)),
+            dma((dps,)), dma((dps,)), dma((3, dps)), dma((3, dps)),
             dma((peers,)), dma((peers,)), dma((peers,)), dma((peers,)),
             dma, dma((radial,)), dma((radial,)),
         ],

time: 66.1 us -> 64.6 us (0.977)
  Pallas kernels: 58.5 us -> 57 us
    pallas_call x1, Pallas kernels: 58.5 us -> 57 us  [on_device(): pl.pallas_call(kernel, out_shape=(shape((radial, azimuth, outs, axial), B...]
where the time goes in v2:
time: 64.6 us; the launch traced here: 64.5 us
  Pallas kernels  57 us (88%)
  local copies, waits for them, and re-layouts  6.8 us (11%)
  between operations  0.65 us (1%)
    pallas_call x1, Pallas kernels, on_device(): pl.pallas_call(kernel, out_shape=(shape((radial, azimuth, outs, axial), B...  57 us
    unnamed x10, local copies, waits for them, and re-layouts  6.8 us

profile of v2, /device:TPU:0, one launch (start us, length us, event | category | flops | bytes accessed | tf_op | source)
XLA Modules:
  0.0 64.5 jit_solution(6805087105811312323)
XLA Ops:
  0.6 57.0 %shard_map.75 = (bf16[4,8,96,256]{3,2,1,0:T(8,128)(2,1)}, bf16[4,8,96,256]{3,2,1,0:T(8,128)(2,1)}, f32[24,2592]{1,0:T(8,128)}, f32[1,24]{1,0:T(1,128)}) custom-call(bf16[96,4,8,256]{3,2,1,0:T(8,128)(2,1)} %bitcast.10, bf16[24,2592]{1,0:T(8,128)(2,1)} %weight.1, bf16[1,24]{1,0:T(2,128)(2,1)} %bitcast.14, bf16[96,4,8,256]{3,2,1,0:T(8,128)(2,1)} %bitcast.11), custom_call_target="tpu_custom_call" | custom-call | tf_op jit(solution)/shard_map/pallas_call | solution.py:391
  57.7 0.0 copy-start
  57.7 3.5 %copy.8 = bf16[1,96,4,8,256]{4,3,2,1,0:T(8,128)(2,1)} copy(bf16[1,96,4,8,256]{4,1,3,2,0:T(8,128)(2,1)} %bitcast.13) | data formatting | bytes 3145728
  61.2 0.0 copy-done
  61.2 0.0 copy-start.1
  61.2 0.0 copy-start.2
  61.2 2.0 %copy.9 = bf16[1,96,4,8,256]{4,3,2,1,0:T(8,128)(2,1)} copy(bf16[1,96,4,8,256]{4,1,3,2,0:T(8,128)(2,1)S(1)} %bitcast.12) | data formatting | bytes 3145728
  63.3 0.0 copy-done.1
  63.3 0.7 %copy.12 = f32[24,2592]{1,0:T(8,128)} copy(f32[24,2592]{1,0:T(8,128)S(1)} %copy-done.1) | data formatting | bytes 497664
  64.0 0.0 copy-done.2
  64.0 0.5 copy.13
Async XLA Ops:
  57.7 3.6 %copy-start = (bf16[4,8,96,256]{3,2,1,0:T(8,128)(2,1)S(1)}, bf16[4,8,96,256]{3,2,1,0:T(8,128)(2,1)}, u32[]{:S(2)}) copy-start(bf16[4,8,96,256]{3,2,1,0:T(8,128)(2,1)} %get-tuple-element.9) | copy-start | bytes 4718596
  61.2 2.0 %copy-start.1 = (f32[24,2592]{1,0:T(8,128)S(1)}, f32[24,2592]{1,0:T(8,128)}, u32[]{:S(2)}) copy-start(f32[24,2592]{1,0:T(8,128)} %get-tuple-element.22) | copy-start | bytes 746500
  61.2 2.7 %copy-start.2 = (f32[1,24]{1,0:T(1,128)S(1)}, f32[1,24]{1,0:T(1,128)}, u32[]{:S(2)}) copy-start(f32[1,24]{1,0:T(1,128)} %get-tuple-element.11) | copy-start | bytes 292

commit v3 on v2

--- a/solution.py
+++ b/solution.py
@@ -86,7 +86,7 @@
         for copy in self.main():
             copy.wait()
 
-    def finish_rim(self):
+    def start_corners(self):
         @pl.when(self.rad > 0)
         def _():
             self.up().wait_recv()
@@ -107,6 +107,7 @@
         def _():
             self.cells[self.radial + 1] = jnp.zeros(self.cells.shape[1:], BF16)
 
+    def wait_corners(self):
         @pl.when(self.rad > 0)
         def _():
             self.down().wait_send()
@@ -231,9 +232,13 @@
     def _(n):
         r = lax.rem(n + 1, radial)
 
+        @pl.when(n == max(radial - 3, 0))
+        def _():
+            halo.start_corners()
+
         @pl.when(n == radial - 2)
         def _():
-            halo.finish_rim()
+            halo.wait_corners()
 
         @pl.loop(0, azimuth // 2)
         def _(pair):
@@ -309,9 +314,13 @@
         r = lax.rem(step // pairs + 1, radial)
         pair = lax.rem(step, pairs)
 
+        @pl.when(step == max(radial - 3, 0) * pairs)
+        def _():
+            dhalo.start_corners()
+
         @pl.when(step == (radial - 2) * pairs)
         def _():
-            dhalo.finish_rim()
+            dhalo.wait_corners()
 
         @pl.when(step == 3 * steps // 8)
         def _():
@@ -375,6 +384,16 @@
     def _(r):
         out_copy(r).wait()
         back_copy(r).wait()
+
+
+def turn_kernel(output, input_grad, weight_grad, bias_grad, output_to, input_to, weight_to, bias_to):
+    output_to[:, 0] = jnp.swapaxes(output[0], 0, 1)
+    input_to[:, 0] = jnp.swapaxes(input_grad[0], 0, 1)
+
+    @pl.when(pl.program_id(0) == 0)
+    def _():
+        weight_to[...] = weight_grad[...]
+        bias_to[...] = bias_grad[...]
 
 
 def on_device(inputs, weight, bias, cotangent):
@@ -427,9 +446,24 @@
             vmem_limit_bytes=VMEM_LIMIT, collective_id=0, has_side_effects=True
         ),
     )(inputs[0], weight, bias[None], cotangent[0])
-    output = output.transpose(2, 0, 1, 3)[None]
-    input_grad = input_grad.transpose(2, 0, 1, 3)[None]
-    return output, input_grad, weight_grad, bias_grad[0]
+    row_in = pl.BlockSpec((1, azimuth, channels, axial), lambda r: (r, 0, 0, 0))
+    row_out = pl.BlockSpec((channels, 1, azimuth, axial), lambda r: (0, r, 0, 0))
+    weight_spec = pl.BlockSpec((rows, depth), lambda r: (0, 0))
+    bias_spec = pl.BlockSpec((1, rows), lambda r: (0, 0))
+    output, input_grad, weight_grad, bias_grad = pl.pallas_call(
+        turn_kernel,
+        grid=(radial,),
+        out_shape=(
+            shape((outs, radial, azimuth, axial), BF16),
+            shape((channels, radial, azimuth, axial), BF16),
+            shape((rows, depth), F32),
+            shape((1, rows), F32),
+        ),
+        in_specs=[row_in, row_in, weight_spec, bias_spec],
+        out_specs=(row_out, row_out, weight_spec, bias_spec),
+        compiler_params=pltpu.CompilerParams(vmem_limit_bytes=63 * 1024 * 1024),
+    )(output, input_grad, weight_grad, bias_grad)
+    return output[None], input_grad[None], weight_grad, bias_grad[0]
 
 
 def solution(mesh):

time: 64.6 us -> 60.8 us (0.941)
  local copies, waits for them, and re-layouts: 6.8 us -> 0 us
  Pallas kernels: 57 us -> 60 us
    unnamed x10 -> x0, local copies, waits for them, and re-layouts: 6.8 us -> none
    pallas_call x0 -> x1, Pallas kernels: none -> 4.62 us  [on_device(): pl.pallas_call(turn_kernel, grid=(radial,), out_shape=(shape((outs, radia...]
    pallas_call x1, Pallas kernels: 57 us -> 55.4 us  [on_device(): pl.pallas_call(kernel, out_shape=(shape((radial, azimuth, outs, axial), B...]
where the time goes in v3:
time: 60.8 us; the launch traced here: 60.6 us
  Pallas kernels  60 us (99%)
  between operations  0.64 us (1%)
    pallas_call x1, Pallas kernels, on_device(): pl.pallas_call(kernel, out_shape=(shape((radial, azimuth, outs, axial), B...  55.4 us
    pallas_call x1, Pallas kernels, on_device(): pl.pallas_call(turn_kernel, grid=(radial,), out_shape=(shape((outs, radia...  4.62 us

profile of v3, /device:TPU:0, one launch (start us, length us, event | category | flops | bytes accessed | tf_op | source)
XLA Modules:
  0.0 60.6 jit_solution(17277241393099206122)
XLA Ops:
  0.6 55.4 %shard_map.75 = (bf16[4,8,96,256]{3,2,1,0:T(8,128)(2,1)}, bf16[4,8,96,256]{3,2,1,0:T(8,128)(2,1)}, f32[24,2592]{1,0:T(8,128)}, f32[1,24]{1,0:T(1,128)}) custom-call(bf16[96,4,8,256]{3,2,1,0:T(8,128)(2,1)} %bitcast.6, bf16[24,2592]{1,0:T(8,128)(2,1)} %weight.1, bf16[1,24]{1,0:T(2,128)(2,1)} %bitcast.8, bf16[96,4,8,256]{3,2,1,0:T(8,128)(2,1)} %bitcast.7), custom_call_target="tpu_custom_call" | custom-call | tf_op jit(solution)/shard_map/pallas_call | solution.py:410
  56.0 4.6 %shard_map.76 = (bf16[96,4,8,256]{3,2,1,0:T(8,128)(2,1)}, bf16[96,4,8,256]{3,2,1,0:T(8,128)(2,1)}, f32[24,2592]{1,0:T(8,128)}, f32[1,24]{1,0:T(1,128)}) custom-call(bf16[4,8,96,256]{3,2,1,0:T(8,128)(2,1)} %get-tuple-element.12.output, bf16[4,8,96,256]{3,2,1,0:T(8,128)(2,1)} %get-tuple-element.13.input_grad, f32[24,2592]{1,0:T(8,128)} %get-tuple-element.14.weight_grad, ...), custom_call_target="tpu_custom_call" | custom-call | tf_op jit(solution)/shard_map/pallas_call | solution.py:453

commit v4 on v3

--- a/solution.py
+++ b/solution.py
@@ -138,6 +138,7 @@
     outs = rows * dps
     block = depth // 27
     width = final.shape[2]
+    batch = max(b for b in (1, 2, 4) if azimuth % b == 0)
     span = (mine.shape[1] - LANES) // 3
 
     def group(k):
@@ -240,10 +241,10 @@
         def _():
             halo.wait_corners()
 
-        @pl.loop(0, azimuth // 2)
-        def _(pair):
-            for p in range(2):
-                a = 2 * pair + p
+        @pl.loop(0, azimuth // batch)
+        def _(part):
+            for p in range(batch):
+                a = batch * part + p
                 preact = convolve(fwd_weight[...], cells, r, a) + bias_column[:, :1]
                 gate = 0.5 * jnp.tanh(0.5 * preact) + 0.5
                 result[r, a] = (preact * gate).astype(BF16)
@@ -306,7 +307,7 @@
         )
 
     dhalo.wait_main()
-    pairs = azimuth // 2
+    pairs = azimuth // batch
     steps = radial * pairs
 
     @pl.loop(0, steps)
@@ -360,8 +361,8 @@
             def _(k):
                 f_copy(k).start()
 
-        for p in range(2):
-            a = 2 * pair + p
+        for p in range(batch):
+            a = batch * pair + p
             back_result[r, a] = convolve(back_weight[...], dcells, r, a).astype(BF16)
 
         @pl.when(pair == pairs - 1)

time: 60.8 us -> 56.4 us (0.928)
  Pallas kernels: 60 us -> 55.6 us
    pallas_call x1, Pallas kernels: 55.4 us -> 50.9 us  [on_device(): pl.pallas_call(kernel, out_shape=(shape((radial, azimuth, outs, axial), B...]
where the time goes in v4:
time: 56.4 us; the launch traced here: 56.2 us
  Pallas kernels  55.6 us (99%)
  between operations  0.64 us (1%)
    pallas_call x1, Pallas kernels, on_device(): pl.pallas_call(kernel, out_shape=(shape((radial, azimuth, outs, axial), B...  50.9 us
    pallas_call x1, Pallas kernels, on_device(): pl.pallas_call(turn_kernel, grid=(radial,), out_shape=(shape((outs, radia...  4.62 us

profile of v4, /device:TPU:0, one launch (start us, length us, event | category | flops | bytes accessed | tf_op | source)
XLA Modules:
  0.0 56.2 jit_solution(17605543287633875153)
XLA Ops:
  0.6 50.9 %shard_map.75 = (bf16[4,8,96,256]{3,2,1,0:T(8,128)(2,1)}, bf16[4,8,96,256]{3,2,1,0:T(8,128)(2,1)}, f32[24,2592]{1,0:T(8,128)}, f32[1,24]{1,0:T(1,128)}) custom-call(bf16[96,4,8,256]{3,2,1,0:T(8,128)(2,1)} %bitcast.6, bf16[24,2592]{1,0:T(8,128)(2,1)} %weight.1, bf16[1,24]{1,0:T(2,128)(2,1)} %bitcast.8, bf16[96,4,8,256]{3,2,1,0:T(8,128)(2,1)} %bitcast.7), custom_call_target="tpu_custom_call" | custom-call | tf_op jit(solution)/shard_map/pallas_call | solution.py:411
  51.6 4.6 %shard_map.76 = (bf16[96,4,8,256]{3,2,1,0:T(8,128)(2,1)}, bf16[96,4,8,256]{3,2,1,0:T(8,128)(2,1)}, f32[24,2592]{1,0:T(8,128)}, f32[1,24]{1,0:T(1,128)}) custom-call(bf16[4,8,96,256]{3,2,1,0:T(8,128)(2,1)} %get-tuple-element.12.output, bf16[4,8,96,256]{3,2,1,0:T(8,128)(2,1)} %get-tuple-element.13.input_grad, f32[24,2592]{1,0:T(8,128)} %get-tuple-element.14.weight_grad, ...), custom_call_target="tpu_custom_call" | custom-call | tf_op jit(solution)/shard_map/pallas_call | solution.py:454
